TPU v7x, 256 devices: a whole 4x4x8 slice. The times are simulated.
256 devices in a mesh: sec: 2 (over core), row: 16 (over x, y), col: 8 (over z).
Axes of the slice: x: 4, y: 4, z: 8, core: 2. Of those that a mesh axis runs over, the one named last changes fastest.
Arguments:
- images: bfloat16 [2, 256, 256, 384], P('sec', 'row', 'col'), may hold values from -6 to 6
- kernel_one: float32 [49, 384], replicated, may hold values from -0.875 to 0.875
- gain_one: float32 [384], replicated, may hold values from 0.5 to 1.5
- shift_one: float32 [384], replicated, may hold values from -3 to 3
- up_one: bfloat16 [384, 1536], P(None, ('sec', 'row', 'col')), may hold values from -0.3125 to 0.3125
- up_bias_one: float32 [1536], replicated, may hold values from -3 to 3
- down_one: bfloat16 [384, 1536], P(None, ('sec', 'row', 'col')), may hold values from -0.15625 to 0.15625
- down_bias_one: float32 [384], replicated, may hold values from -3 to 3
- scale_one: float32 [384], replicated, may hold values from 0.3 to 1.5
- gain_mid: float32 [384], replicated, may hold values from 0.5 to 1.5
- shift_mid: float32 [384], replicated, may hold values from -3 to 3
- merge_weight: bfloat16 [1536, 768], replicated, may hold values from -0.15625 to 0.15625
- merge_bias: float32 [768], replicated, may hold values from -3 to 3
- kernel_two: float32 [49, 768], replicated, may hold values from -0.875 to 0.875
- gain_two: float32 [768], replicated, may hold values from 0.5 to 1.5
- shift_two: float32 [768], replicated, may hold values from -3 to 3
- up_two: bfloat16 [768, 3072], P(None, ('sec', 'row', 'col')), may hold values from -0.21875 to 0.21875
- up_bias_two: float32 [3072], replicated, may hold values from -3 to 3
- down_two: bfloat16 [768, 3072], P(None, ('sec', 'row', 'col')), may hold values from -0.109375 to 0.109375
- down_bias_two: float32 [768], replicated, may hold values from -3 to 3
- scale_two: float32 [768], replicated, may hold values from 0.3 to 1.5
- grad_out: bfloat16 [2, 128, 128, 768], P('sec', 'row', 'col'), may hold values from -6 to 6
Outputs:
- features: bfloat16 [2, 128, 128, 768], P('sec', 'row', 'col')
- input_grad: bfloat16 [2, 256, 256, 384], P('sec', 'row', 'col')
All inputs are finite; a program needn't handle non-finite values.
Results may differ from a plain program's by a relative error of at most 0.02.
Values may be sent and summed in bfloat16 or wider, within the bound.
No kernel may reach another device: no remote copies, remote signals or barrier semaphores. Data moves between devices by JAX's collectives and lax.ppermute only.
A program may use at most 128 MiB of HBM per device.

v0:
```python
import jax
import jax.numpy as jnp
from jax import lax
from jax.sharding import PartitionSpec as P

norm_eps = 1e-06


def with_halo(block, sides, width):
    for axis, dim in sides:
        count = lax.axis_size(axis)
        forward = [(i, i + 1) for i in range(count - 1)]
        backward = [(target, source) for source, target in forward]
        low = lax.ppermute(
            lax.slice_in_dim(block, block.shape[dim] - width, None, axis=dim), axis, forward
        )
        high = lax.ppermute(lax.slice_in_dim(block, 0, width, axis=dim), axis, backward)
        block = jnp.concatenate([low, block, high], axis=dim)
    return block


def gelu_exact(values):
    return 0.5 * values * (1.0 + lax.erf(values * 0.7071067811865476))


def gelu_slope(values):
    return (
        0.5 * (1.0 + lax.erf(values * 0.7071067811865476))
        + values * jnp.exp(-0.5 * values * values) * 0.3989422804014327
    )


def norm_forward(values, norm_gain, norm_shift):
    center = values - jnp.mean(values, axis=-1, keepdims=True)
    inv_std = lax.rsqrt(jnp.mean(center * center, axis=-1, keepdims=True) + norm_eps)
    scaled = center * inv_std
    return (scaled, inv_std, scaled * norm_gain + norm_shift)


def norm_backward(upstream, scaled, inv_std, norm_gain):
    weighted = upstream * norm_gain
    mean_one = jnp.mean(weighted, axis=-1, keepdims=True)
    mean_two = jnp.mean(weighted * scaled, axis=-1, keepdims=True)
    return inv_std * (weighted - mean_one - scaled * mean_two)


def taps_last(padded, kernel, row_count, col_count, flipped):
    summed = jnp.zeros(padded.shape[:-3] + (row_count, col_count, padded.shape[-1]), jnp.float32)
    for tap_index in range(49):
        row_off = tap_index // 7
        col_off = tap_index % 7
        if flipped:
            row_off = 6 - row_off
            col_off = 6 - col_off
        summed = (
            summed
            + padded[..., row_off : row_off + row_count, col_off : col_off + col_count, :]
            * kernel[tap_index]
        )
    return summed


def taps_first(padded, kernel, row_count, col_count, flipped):
    summed = jnp.zeros(padded.shape[:-2] + (row_count, col_count), jnp.float32)
    for tap_index in range(49):
        row_off = tap_index // 7
        col_off = tap_index % 7
        if flipped:
            row_off = 6 - row_off
            col_off = 6 - col_off
        summed = (
            summed
            + padded[..., row_off : row_off + row_count, col_off : col_off + col_count]
            * kernel[tap_index][:, None, None, None]
        )
    return summed


def contract_last(left_side, right_side):
    return lax.dot_general(
        left_side, right_side, (((1,), (1,)), ((), ())), preferred_element_type=jnp.float32
    )


def dense_forward(normed, up_full, down_full, up_bias, down_bias):
    pre_act = jnp.dot(normed, up_full, preferred_element_type=jnp.float32) + up_bias
    hidden = gelu_exact(pre_act).astype(jnp.bfloat16)
    return (contract_last(hidden, down_full) + down_bias, pre_act)


def dense_backward(d_branch, pre_act, up_full, down_full):
    d_hidden = jnp.dot(d_branch, down_full, preferred_element_type=jnp.float32)
    d_pre = (d_hidden * gelu_slope(pre_act)).astype(jnp.bfloat16)
    return contract_last(d_pre, up_full)


def with_rims(tile_values):
    return with_halo(tile_values, (("row", 1), ("col", 2)), 3)


def regroup(blocks):
    moved = lax.all_to_all(blocks, ("row", "col"), split_axis=0, concat_axis=0, tiled=True)
    return moved


def on_device(
    images,
    kernel_one,
    gain_one,
    shift_one,
    up_one,
    up_bias_one,
    down_one,
    down_bias_one,
    scale_one,
    gain_mid,
    shift_mid,
    merge_weight,
    merge_bias,
    kernel_two,
    gain_two,
    shift_two,
    up_two,
    up_bias_two,
    down_two,
    down_bias_two,
    scale_two,
    grad_out,
):
    micro_count, tile_rows, tile_cols, width_one = images.shape
    width_two = merge_weight.shape[1]
    grid_rows = lax.axis_size("row")
    grid_cols = lax.axis_size("col")
    groups = grid_rows * grid_cols
    per_group = width_two // groups
    half_rows = tile_rows // 2
    half_cols = tile_cols // 2
    tile_pos = half_rows * half_cols
    full_rows = half_rows * grid_rows
    full_cols = half_cols * grid_cols
    rows_one = micro_count * tile_rows * tile_cols
    rows_two = micro_count * tile_pos
    frame_pads = ((0, 0), (0, 0), (3, 3), (3, 3))

    def to_channels(row_values):
        outgoing = row_values.reshape(micro_count, tile_pos, groups, per_group).transpose(
            2, 3, 0, 1
        )
        arrived = regroup(outgoing)
        picture = arrived.reshape(
            grid_rows, grid_cols, per_group, micro_count, half_rows, half_cols
        )
        return picture.transpose(2, 3, 0, 4, 1, 5).reshape(
            per_group, micro_count, full_rows, full_cols
        )

    def to_tiles(picture):
        outgoing = picture.reshape(
            per_group, micro_count, grid_rows, half_rows, grid_cols, half_cols
        )
        outgoing = outgoing.transpose(2, 4, 0, 1, 3, 5).reshape(
            groups, per_group, micro_count, tile_pos
        )
        arrived = regroup(outgoing)
        return arrived.transpose(2, 3, 0, 1).reshape(rows_two, width_two)

    gathered = (
        lax.all_gather(up_one, ("sec", "row", "col"), axis=1, tiled=True),
        lax.all_gather(down_one, ("sec", "row", "col"), axis=1, tiled=True),
        lax.all_gather(up_two, ("sec", "row", "col"), axis=1, tiled=True),
        lax.all_gather(down_two, ("sec", "row", "col"), axis=1, tiled=True),
    )
    pair_one = (gathered[0], gathered[1])
    pair_two = (gathered[2], gathered[3])

    def project_forward(normed, weight_pair, up_bias, down_bias):
        branch, pre_act = dense_forward(normed, weight_pair[0], weight_pair[1], up_bias, down_bias)
        return (branch, pre_act)

    def project_backward(d_branch, pre_act, weight_pair):
        result = dense_backward(d_branch, pre_act, weight_pair[0], weight_pair[1])
        return result

    padded_one = with_rims(images).astype(jnp.float32)
    conv_one = taps_last(padded_one, kernel_one, tile_rows, tile_cols, False).reshape(
        rows_one, width_one
    )
    scaled_one, inv_one, normed_one = norm_forward(conv_one, gain_one, shift_one)
    normed_one = normed_one.astype(jnp.bfloat16)
    branch_one, pre_one = project_forward(normed_one, pair_one, up_bias_one, down_bias_one)
    section_out = (
        images.reshape(rows_one, width_one).astype(jnp.float32) + scale_one * branch_one
    ).astype(jnp.bfloat16)
    scaled_mid, inv_mid, normed_mid = norm_forward(
        section_out.astype(jnp.float32), gain_mid, shift_mid
    )
    patches = normed_mid.astype(jnp.bfloat16).reshape(
        micro_count, half_rows, 2, half_cols, 2, width_one
    )
    patches = patches.transpose(0, 1, 3, 2, 4, 5).reshape(rows_two, 4 * width_one)
    merged = (
        jnp.dot(patches, merge_weight, preferred_element_type=jnp.float32) + merge_bias
    ).astype(jnp.bfloat16)
    group_index = lax.axis_index(("row", "col"))
    kernel_part = lax.dynamic_slice_in_dim(kernel_two, group_index * per_group, per_group, 1)
    picture = to_channels(merged)
    padded_two = jnp.pad(picture.astype(jnp.float32), frame_pads)
    conv_picture = taps_first(padded_two, kernel_part, full_rows, full_cols, False).astype(
        jnp.bfloat16
    )
    conv_two = to_tiles(conv_picture)
    scaled_two, inv_two, normed_two = norm_forward(
        conv_two.astype(jnp.float32), gain_two, shift_two
    )
    normed_two = normed_two.astype(jnp.bfloat16)
    branch_two, pre_two = project_forward(normed_two, pair_two, up_bias_two, down_bias_two)
    features = (merged.astype(jnp.float32) + scale_two * branch_two).astype(jnp.bfloat16)
    grad_rows = grad_out.reshape(rows_two, width_two)
    d_branch_two = (grad_rows.astype(jnp.float32) * scale_two).astype(jnp.bfloat16)
    d_normed_two = project_backward(d_branch_two, pre_two, pair_two)
    d_conv_two = norm_backward(d_normed_two, scaled_two, inv_two, gain_two).astype(jnp.bfloat16)
    back_picture = to_channels(d_conv_two)
    padded_back = jnp.pad(back_picture.astype(jnp.float32), frame_pads)
    d_taps = to_tiles(
        taps_first(padded_back, kernel_part, full_rows, full_cols, True).astype(jnp.bfloat16)
    )
    d_taps = lax.optimization_barrier(d_taps).astype(jnp.float32)
    d_merged = (d_taps + grad_rows.astype(jnp.float32)).astype(jnp.bfloat16)
    d_patches = contract_last(d_merged, merge_weight)
    d_normed_mid = d_patches.reshape(micro_count, half_rows, half_cols, 2, 2, width_one)
    d_normed_mid = d_normed_mid.transpose(0, 1, 3, 2, 4, 5).reshape(rows_one, width_one)
    upstream_one = norm_backward(d_normed_mid, scaled_mid, inv_mid, gain_mid)
    d_branch_one = (upstream_one * scale_one).astype(jnp.bfloat16)
    d_normed_one = project_backward(d_branch_one, pre_one, pair_one)
    d_conv_one = norm_backward(d_normed_one, scaled_one, inv_one, gain_one).astype(jnp.bfloat16)
    d_conv_one = d_conv_one.reshape(micro_count, tile_rows, tile_cols, width_one)
    padded_grad = with_rims(d_conv_one).astype(jnp.float32)
    back_one = taps_last(padded_grad, kernel_one, tile_rows, tile_cols, True).reshape(
        rows_one, width_one
    )
    input_grad = (back_one + upstream_one).astype(jnp.bfloat16).reshape(images.shape)
    return (features.reshape(micro_count, half_rows, half_cols, width_two), input_grad)


def solution(mesh):
    in_specs = (
        P("sec", "row", "col", None),
        P(),
        P(),
        P(),
        P(None, ("sec", "row", "col")),
        P(),
        P(None, ("sec", "row", "col")),
        P(),
        P(),
        P(),
        P(),
        P(),
        P(),
        P(),
        P(),
        P(),
        P(None, ("sec", "row", "col")),
        P(),
        P(None, ("sec", "row", "col")),
        P(),
        P(),
        P("sec", "row", "col", None),
    )
    out_specs = (P("sec", "row", "col", None), P("sec", "row", "col", None))
    return jax.shard_map(
        on_device, mesh=mesh, in_specs=in_specs, out_specs=out_specs, check_vma=False
    )
```

profile of v0, /device:TPU:2, one launch (start us, length us, event | category | flops | bytes accessed | tf_op | source)
XLA Modules:
  0.0 609.3 jit_solution(4079319393452505328)
XLA Ops:
  14.4 4.5 collective-permute-start.1
  24.2 4.5 collective-permute-start.2
  31.3 6.5 %fusion.345 = (f32[16,32]{1,0:T(8,128)S(1)}, f32[1,16,32,384]{3,2,1,0:T(8,128)S(1)}) fusion(f32[384]{0:T(512)} %get-tuple-element.53, f32[1,22,38,384]{3,2,1,0:T(8,128)S(1)} %maximum_convert_fusion, f32[384]{0:T(512)} %get-tuple-element.54, f32[384]{0:T(512)S(1)} %get-tuple-element.7, f32[384]{0:T(512)S(1)} %get-tuple-element.8, ...), kind=kLoop, calls=%fused_computation.691 | loop fusion | flops 19267072 | bytes 39398912 | tf_op jit(solution)/shard_map/reduce_sum | solution.py:34
  39.2 78.0 %all-gather.11.cloned.1.call-done = bf16[256,6,384]{2,1,0:T(8,128)(2,1)} async-done(((bf16[1,6,384]{2,1,0:T(8,128)(2,1)}), bf16[256,6,384]{2,1,0:T(8,128)(2,1)}) %all-gather.11.cloned.1.call-update) | async-done | bytes 1179664 | tf_op jit(solution)/shard_map/all_gather | solution.py:169
  120.5 102.1 %all-gather.9.cloned.1.call-done = bf16[256,6,384]{2,1,0:T(8,128)(2,1)} async-done(((bf16[1,6,384]{2,1,0:T(8,128)(2,1)}), bf16[256,6,384]{2,1,0:T(8,128)(2,1)}) %all-gather.9.cloned.1.call-update) | async-done | bytes 1179664 | tf_op jit(solution)/shard_map/all_gather | solution.py:168
  237.1 12.5 %all-to-all-start = ((bf16[128,6,1,128]{3,1,2,0:T(8,128)(2,1)}), bf16[128,6,1,128]{3,1,2,0:T(8,128)(2,1)}, u32[]{:S(2)}, u32[]{:S(2)}) async-start(bf16[128,6,1,128]{3,1,2,0:T(8,128)(2,1)} %bitcast.215), calls=%async_computation | async-start | bytes 524288 | tf_op jit(solution)/shard_map/all_to_all | solution.py:102
  255.0 7.6 %all-to-all-done = bf16[128,6,1,128]{3,1,2,0:T(8,128)(2,1)} async-done(((bf16[128,6,1,128]{3,1,2,0:T(8,128)(2,1)}), bf16[128,6,1,128]{3,1,2,0:T(8,128)(2,1)}, u32[]{:S(2)}, u32[]{:S(2)}) %all-to-all-start) | async-done | bytes 196640 | tf_op jit(solution)/shard_map/all_to_all | solution.py:102
  274.2 6.7 %fusion.222 = bf16[6,1,128,128]{3,2,0,1:T(8,128)(2,1)} fusion(f32[6,1,128,128]{3,2,0,1:T(8,128)S(1)} %reshape.616, f32[6]{0:T(128)} %get-tuple-element.113, f32[6]{0:T(128)} %get-tuple-element.66, f32[6]{0:T(128)} %get-tuple-element.67, f32[6]{0:T(128)} %get-tuple-element.68, f32[6]{0:T(128)} %get-tuple-element.69, f32[6]{0:T(128)} %get-tuple-element.70, ...), kind=kLoop, calls=%fused_computation.450 | loop fusion | flops 9633792 | bytes 591000 | tf_op jit(solution)/shard_map/convert_element_type | solution.py:208
  289.8 21.1 %all_to_all.20 = bf16[128,6,1,128]{3,1,2,0:T(8,128)(2,1)S(1)} all-to-all(bf16[128,6,1,128]{3,1,2,0:T(8,128)(2,1)} %reshape.630), channel_id=1, replica_groups=mesh['sec'=2,'row'=16,'col'=8] {'row','col'}, dimensions={0} | all-to-all | bytes 393216 | tf_op jit(solution)/shard_map/all_to_all | solution.py:102
  316.8 25.0 %all-gather.13.cloned.1.call-done = bf16[256,12,768]{2,1,0:T(8,128)(2,1)} async-done(((bf16[1,12,768]{2,1,0:T(8,128)(2,1)}), bf16[256,12,768]{2,1,0:T(8,128)(2,1)}) %all-gather.13.cloned.1.call-update) | async-done | bytes 4718608 | tf_op jit(solution)/shard_map/all_gather | solution.py:170
  341.7 8.4 %reshape.627 = bf16[3072,768]{1,0:T(8,128)(2,1)} reshape(bf16[256,12,768]{2,1,0:T(8,128)(2,1)} %all-gather.13.cloned.1.call-done) | data formatting | bytes 9437184
  350.2 5.2 convolution_add_fusion
  355.4 103.5 %all-gather.15.cloned.1.call-done = bf16[256,12,768]{2,1,0:T(8,128)(2,1)} async-done(((bf16[1,12,768]{2,1,0:T(8,128)(2,1)}), bf16[256,12,768]{2,1,0:T(8,128)(2,1)}) %all-gather.15.cloned.1.call-update) | async-done | bytes 4718608 | tf_op jit(solution)/shard_map/all_gather | solution.py:171
  458.9 8.4 %reshape.629 = bf16[3072,768]{1,0:T(8,128)(2,1)} reshape(bf16[256,12,768]{2,1,0:T(8,128)(2,1)} %all-gather.15.cloned.1.call-done) | data formatting | bytes 9437184
  467.2 7.9 %fusion.344 = (f32[128]{0:T(128)}, f32[128]{0:T(128)}, f32[128,768]{1,0:T(8,128)}) fusion(f32[128]{0:T(128)} %add_rsqrt_fusion.2, f32[128,768]{1,0:T(8,128)S(1)} %copy-done.6, f32[128]{0:T(128)} %copy-done.94, f32[768]{0:T(1024)} %param.36, bf16[3072,768]{1,0:T(8,128)(2,1)} %reshape.627, bf16[3072,768]{1,0:T(8,128)(2,1)} %reshape.629, ...), kind=kOutput, calls=%fused_computation.690 | convolution fusion | flops 1212776192 | bytes 12001280 | tf_op jit(solution)/shard_map/dot_general | solution.py:80
  480.4 23.5 %all_to_all.21 = bf16[128,6,1,128]{3,1,2,0:T(8,128)(2,1)S(1)} all-to-all(bf16[128,6,1,128]{3,1,2,0:T(8,128)(2,1)S(1)} %bitcast.216), channel_id=1, replica_groups=mesh['sec'=2,'row'=16,'col'=8] {'row','col'}, dimensions={0} | all-to-all | bytes 393216 | tf_op jit(solution)/shard_map/all_to_all | solution.py:102
  506.6 4.4 copy.74
  513.4 6.7 %fusion.319 = bf16[6,1,128,128]{3,2,0,1:T(8,128)(2,1)} fusion(f32[6,1,128,128]{3,2,0,1:T(8,128)S(1)} %reshape.619, f32[6]{0:T(128)} %get-tuple-element.113, f32[6]{0:T(128)} %get-tuple-element.66, f32[6]{0:T(128)} %get-tuple-element.67, f32[6]{0:T(128)} %get-tuple-element.68, f32[6]{0:T(128)} %get-tuple-element.69, f32[6]{0:T(128)} %get-tuple-element.70, ...), kind=kLoop, calls=%fused_computation.547 | loop fusion | flops 9633792 | bytes 591000 | tf_op jit(solution)/shard_map/convert_element_type | solution.py:225
  528.4 21.0 %all_to_all.22 = bf16[128,6,1,128]{3,1,2,0:T(8,128)(2,1)} all-to-all(bf16[128,6,1,128]{3,1,2,0:T(8,128)(2,1)S(1)} %reshape.631), channel_id=1, replica_groups=mesh['sec'=2,'row'=16,'col'=8] {'row','col'}, dimensions={0} | all-to-all | bytes 393216 | tf_op jit(solution)/shard_map/all_to_all | solution.py:102
  563.0 6.3 %fusion.343 = (f32[512]{0:T(512)S(1)}, f32[512]{0:T(512)S(1)}, f32[512,384]{1,0:T(8,128)}) fusion(f32[512]{0:T(512)S(1)} %copy-done.92, f32[512]{0:T(512)S(1)} %copy-done.90, f32[1,16,32,384]{3,2,1,0:T(8,128)} %copy-done.1, f32[384]{0:T(512)S(1)} %copy-done.100, bf16[1536,384]{1,0:T(8,128)(2,1)} %copy-done.5, f32[512,1536]{1,0:T(8,128)} %copy-done.7, ...), kind=kOutput, calls=%fused_computation.689 | convolution fusion | flops 1218771968 | bytes 8671744 | tf_op jit(solution)/shard_map/dot_general | solution.py:80
  571.2 4.3 collective-permute-start.5
  577.5 6.4 %collective-permute-done.4 = bf16[1,3,32,384]{3,2,1,0:T(8,128)(2,1)S(1)} collective-permute-done((bf16[1,3,32,384]{3,2,1,0:T(8,128)(2,1)S(1)}, bf16[1,3,32,384]{3,2,1,0:T(8,128)(2,1)S(1)}, u32[]{:S(2)}, u32[]{:S(2)}) %collective-permute-start.4) | collective-permute-done | bytes 73760 | tf_op jit(solution)/shard_map/ppermute | solution.py:14
  585.3 4.5 collective-permute-start.6
  594.9 6.3 %fusion.23 = f32[1,16,32,384]{3,2,1,0:T(8,128)S(1)} fusion(f32[1,22,38,384]{3,2,1,0:T(8,128)S(1)} %maximum_convert_fusion.1, f32[384]{0:T(512)} %get-tuple-element.53, f32[384]{0:T(512)} %get-tuple-element.54, f32[384]{0:T(512)S(1)} %copy-done.14, f32[384]{0:T(512)S(1)} %copy-done.16, f32[384]{0:T(512)S(1)} %copy-done.18, f32[384]{0:T(512)S(1)} %copy-done.20, ...), kind=kLoop, calls=%fused_computation.133 | loop fusion | flops 19070976 | bytes 39396864 | tf_op jit(solution)/shard_map/add | solution.py:56
  (302 shorter events, 108.1 us)
Async XLA Ops:
  7.2 227.5 %copy-start = (bf16[1536,768]{1,0:T(8,128)(2,1)S(1)}, bf16[1536,768]{1,0:T(8,128)(2,1)}, u32[]{:S(2)}) copy-start(bf16[1536,768]{1,0:T(8,128)(2,1)} %param.33) | copy-start | bytes 7077892
  7.2 110.1 %all-gather.11.cloned.1.call-start = ((), (), s32[]{:S(2)}) async-start(), calls=%async_computation.5 | async-start | bytes 1579008 | tf_op jit(solution)/shard_map/all_gather | solution.py:169
  7.9 214.7 %all-gather.9.cloned.1.call-start = ((), (), s32[]{:S(2)}) async-start(), calls=%async_computation.4 | async-start | bytes 1579008 | tf_op jit(solution)/shard_map/all_gather | solution.py:168
  8.7 333.1 %all-gather.13.cloned.1.call-start = ((), (), s32[]{:S(2)}) async-start(), calls=%async_computation.6 | async-start | bytes 6316032 | tf_op jit(solution)/shard_map/all_gather | solution.py:170
  9.4 449.5 %all-gather.15.cloned.1.call-start = ((), (), s32[]{:S(2)}) async-start(), calls=%async_computation.7 | async-start | bytes 6316032 | tf_op jit(solution)/shard_map/all_gather | solution.py:171
  10.9 10.8 %collective-permute-start = (bf16[1,3,32,384]{3,2,1,0:T(8,128)(2,1)S(1)}, bf16[1,3,32,384]{3,2,1,0:T(8,128)(2,1)S(1)}, u32[]{:S(2)}, u32[]{:S(2)}) collective-permute-start(bf16[1,3,32,384]{3,2,1,0:T(8,128)(2,1)S(1)} %get-tuple-element.64), channel_id=1, source_target_pairs={{0,8},{8,16},{16,24},{24,32},{32,40},{40,48},{48,56},{56,64},{64,7... | collective-permute-start | bytes 221192 | tf_op jit(solution)/shard_map/ppermute | solution.py:14
  14.4 8.4 %collective-permute-start.1 = (bf16[1,3,32,384]{3,2,1,0:T(8,128)(2,1)S(1)}, bf16[1,3,32,384]{3,2,1,0:T(8,128)(2,1)S(1)}, u32[]{:S(2)}, u32[]{:S(2)}) collective-permute-start(bf16[1,3,32,384]{3,2,1,0:T(8,128)(2,1)S(1)} %get-tuple-element.63), channel_id=1, source_target_pairs={{8,0},{16,8},{24,16},{32,24},{40,32},{48,40},{56,48},{64,56},{72,6... | collective-permute-start | bytes 221192 | tf_op jit(solution)/shard_map/ppermute | solution.py:17
  22.9 7.5 %collective-permute-start.3 = (bf16[1,22,3,384]{3,2,1,0:T(4,128)(2,1)S(1)}, bf16[1,22,3,384]{3,2,1,0:T(4,128)(2,1)S(1)}, u32[]{:S(2)}, u32[]{:S(2)}) collective-permute-start(bf16[1,22,3,384]{3,2,1,0:T(4,128)(2,1)S(1)} %get-tuple-element.60), channel_id=1, source_target_pairs={{1,0},{2,1},{3,2},{4,3},{5,4},{6,5},{7,6},{9,8},{10,9},{11,10},{12... | collective-permute-start | bytes 152072 | tf_op jit(solution)/shard_map/ppermute | solution.py:17
  24.2 6.5 %collective-permute-start.2 = (bf16[1,22,3,384]{3,2,1,0:T(4,128)(2,1)S(1)}, bf16[1,22,3,384]{3,2,1,0:T(4,128)(2,1)S(1)}, u32[]{:S(2)}, u32[]{:S(2)}) collective-permute-start(bf16[1,22,3,384]{3,2,1,0:T(4,128)(2,1)S(1)} %get-tuple-element.59), channel_id=1, source_target_pairs={{0,1},{1,2},{2,3},{3,4},{4,5},{5,6},{6,7},{8,9},{9,10},{10,11},{11... | collective-permute-start | bytes 152072 | tf_op jit(solution)/shard_map/ppermute | solution.py:14
  37.8 82.7 %copy-start.1 = (f32[1,16,32,384]{3,2,1,0:T(8,128)}, f32[1,16,32,384]{3,2,1,0:T(8,128)S(1)}, u32[]{:S(2)}) copy-start(f32[1,16,32,384]{3,2,1,0:T(8,128)S(1)} %get-tuple-element.56) | copy-start | bytes 2359300
  37.9 82.6 %copy-start.89 = (f32[512]{0:T(512)}, f32[512]{0:T(512)S(1)}, u32[]{:S(2)}) copy-start(f32[512]{0:T(512)S(1)} %div.41) | copy-start | bytes 6148
  38.3 82.3 %copy-start.91 = (f32[512]{0:T(512)}, f32[512]{0:T(512)S(1)}, u32[]{:S(2)}) copy-start(f32[512]{0:T(512)S(1)} %rsqrt.28) | copy-start | bytes 6148
  120.5 104.4 %copy-start.93 = (f32[1536]{0:T(1024)S(1)}, f32[1536]{0:T(1024)}, u32[]{:S(2)}) copy-start(f32[1536]{0:T(1024)} %param.27) | copy-start | bytes 18436
  236.1 31.3 %copy-start.8 = (bf16[128,768]{1,0:T(8,128)(2,1)}, bf16[128,768]{1,0:T(8,128)(2,1)S(1)}, u32[]{:S(2)}) copy-start(bf16[128,768]{1,0:T(8,128)(2,1)S(1)} %fusion.22) | copy-start | bytes 589828
  237.1 25.5 %all-to-all-start = ((bf16[128,6,1,128]{3,1,2,0:T(8,128)(2,1)}), bf16[128,6,1,128]{3,1,2,0:T(8,128)(2,1)}, u32[]{:S(2)}, u32[]{:S(2)}) async-start(bf16[128,6,1,128]{3,1,2,0:T(8,128)(2,1)} %bitcast.215), calls=%async_computation | async-start | bytes 524288 | tf_op jit(solution)/shard_map/all_to_all | solution.py:102
  316.8 33.4 %copy-start.6 = (f32[128,768]{1,0:T(8,128)S(1)}, f32[128,768]{1,0:T(8,128)}, u32[]{:S(2)}) copy-start(f32[128,768]{1,0:T(8,128)} %copy.70) | copy-start | bytes 1179652
  569.3 20.5 %copy-start.4 = (f32[128,3072]{1,0:T(8,128)S(1)}, f32[128,3072]{1,0:T(8,128)}, u32[]{:S(2)}) copy-start(f32[128,3072]{1,0:T(8,128)} %convolution_add_fusion) | copy-start | bytes 4718596
  569.3 20.5 %copy-start.9 = (bf16[128,768]{1,0:T(8,128)(2,1)S(1)}, bf16[128,768]{1,0:T(8,128)(2,1)}, u32[]{:S(2)}) copy-start(bf16[128,768]{1,0:T(8,128)(2,1)} %copy-done.8) | copy-start | bytes 589828
  569.3 20.6 %copy-start.95 = (f32[768]{0:T(1024)S(1)}, f32[768]{0:T(1024)}, u32[]{:S(2)}) copy-start(f32[768]{0:T(1024)} %param.41) | copy-start | bytes 9220
  569.3 20.6 %copy-start.96 = (f32[768]{0:T(1024)S(1)}, f32[768]{0:T(1024)}, u32[]{:S(2)}) copy-start(f32[768]{0:T(1024)} %param.42) | copy-start | bytes 9220
  571.2 6.3 %collective-permute-start.5 = (bf16[1,3,32,384]{3,2,1,0:T(8,128)(2,1)S(1)}, bf16[1,3,32,384]{3,2,1,0:T(8,128)(2,1)S(1)}, u32[]{:S(2)}, u32[]{:S(2)}) collective-permute-start(bf16[1,3,32,384]{3,2,1,0:T(8,128)(2,1)S(1)} %get-tuple-element.62), channel_id=1, source_target_pairs={{8,0},{16,8},{24,16},{32,24},{40,32},{48,40},{56,48},{64,56},{72,6... | collective-permute-start | bytes 221192 | tf_op jit(solution)/shard_map/ppermute | solution.py:17
  575.6 8.4 %collective-permute-start.4 = (bf16[1,3,32,384]{3,2,1,0:T(8,128)(2,1)S(1)}, bf16[1,3,32,384]{3,2,1,0:T(8,128)(2,1)S(1)}, u32[]{:S(2)}, u32[]{:S(2)}) collective-permute-start(bf16[1,3,32,384]{3,2,1,0:T(8,128)(2,1)S(1)} %get-tuple-element.61), channel_id=1, source_target_pairs={{0,8},{8,16},{16,24},{24,32},{32,40},{40,48},{48,56},{56,64},{64,7... | collective-permute-start | bytes 221192 | tf_op jit(solution)/shard_map/ppermute | solution.py:14
  584.0 10.2 %collective-permute-start.7 = (bf16[1,22,3,384]{3,2,1,0:T(4,128)(2,1)S(1)}, bf16[1,22,3,384]{3,2,1,0:T(4,128)(2,1)S(1)}, u32[]{:S(2)}, u32[]{:S(2)}) collective-permute-start(bf16[1,22,3,384]{3,2,1,0:T(4,128)(2,1)S(1)} %get-tuple-element.58), channel_id=1, source_target_pairs={{1,0},{2,1},{3,2},{4,3},{5,4},{6,5},{7,6},{9,8},{10,9},{11,10},{12... | collective-permute-start | bytes 152072 | tf_op jit(solution)/shard_map/ppermute | solution.py:17
  585.3 8.9 %collective-permute-start.6 = (bf16[1,22,3,384]{3,2,1,0:T(4,128)(2,1)S(1)}, bf16[1,22,3,384]{3,2,1,0:T(4,128)(2,1)S(1)}, u32[]{:S(2)}, u32[]{:S(2)}) collective-permute-start(bf16[1,22,3,384]{3,2,1,0:T(4,128)(2,1)S(1)} %get-tuple-element.57), channel_id=1, source_target_pairs={{0,1},{1,2},{2,3},{3,4},{4,5},{5,6},{6,7},{8,9},{9,10},{10,11},{11... | collective-permute-start | bytes 152072 | tf_op jit(solution)/shard_map/ppermute | solution.py:14
  (93 other events, 466.1 us)
Sparse Core Ops, SparseCore 0:
  11.6 105.6 all-gather.10
  120.8 101.8 all-gather.8
  226.5 115.2 all-gather.12
  345.4 113.3 all-gather.14
where the time goes:
time: 619 us; the launch traced here: 609 us
  waiting for transfers between devices  325 us (53%)
  local copies, waits for them, and re-layouts  92.8 us (15%)
  blocking collectives  65.6 us (11%)
  other arithmetic  39.9 us (6%)
  starting transfers between devices  38.6 us (6%)
  matrix products  31.2 us (5%)
  between operations  15.8 us (3%)
    all_gather x1, waiting for transfers between devices, on_device(): lax.all_gather(down_two, ('sec', 'row', 'col'), axis=1, tiled=True)  103 us
    all_gather x1, waiting for transfers between devices, on_device(): lax.all_gather(up_one, ('sec', 'row', 'col'), axis=1, tiled=True)  102 us
    all_gather x1, waiting for transfers between devices, on_device(): lax.all_gather(down_one, ('sec', 'row', 'col'), axis=1, tiled=True)  78 us
    all_to_all x3, blocking collectives, regroup(): lax.all_to_all(blocks, ('row', 'col'), split_axis=0, concat_axis=0, tiled...  65.6 us
    unnamed x214, local copies, waits for them, and re-layouts  25.2 us
    all_gather x1, waiting for transfers between devices, on_device(): lax.all_gather(up_two, ('sec', 'row', 'col'), axis=1, tiled=True)  25 us
    dot_general x5, matrix products, contract_last(): lax.dot_general(left_side, right_side, (((1,), (1,)), ((), ())), preferre...  22.1 us
    ppermute x4, starting transfers between devices, with_halo(): lax.ppermute(lax.slice_in_dim(block, block.shape[dim] - width, None, axis...  14.5 us
  transfers between devices with their start and end apart: 13, of which 7 were waited for; matrix products, arithmetic and copies ran while one was open for 14% of the time, Pallas kernels for 0%

commit v1 on v0

v1 whole, which is shorter than its diff:
```python
import jax
import jax.numpy as jnp
from jax import lax
from jax.sharding import PartitionSpec as P

norm_eps = 1e-06


def with_halo(block, sides, width):
    for axis, dim in sides:
        count = lax.axis_size(axis)
        forward = [(i, i + 1) for i in range(count - 1)]
        backward = [(target, source) for source, target in forward]
        low = lax.ppermute(
            lax.slice_in_dim(block, block.shape[dim] - width, None, axis=dim), axis, forward
        )
        high = lax.ppermute(lax.slice_in_dim(block, 0, width, axis=dim), axis, backward)
        block = jnp.concatenate([low, block, high], axis=dim)
    return block


def gelu_exact(values):
    return 0.5 * values * (1.0 + lax.erf(values * 0.7071067811865476))


def gelu_slope(values):
    return (
        0.5 * (1.0 + lax.erf(values * 0.7071067811865476))
        + values * jnp.exp(-0.5 * values * values) * 0.3989422804014327
    )


def norm_forward(values, norm_gain, norm_shift):
    center = values - jnp.mean(values, axis=-1, keepdims=True)
    inv_std = lax.rsqrt(jnp.mean(center * center, axis=-1, keepdims=True) + norm_eps)
    scaled = center * inv_std
    return (scaled, inv_std, scaled * norm_gain + norm_shift)


def norm_backward(upstream, scaled, inv_std, norm_gain):
    weighted = upstream * norm_gain
    mean_one = jnp.mean(weighted, axis=-1, keepdims=True)
    mean_two = jnp.mean(weighted * scaled, axis=-1, keepdims=True)
    return inv_std * (weighted - mean_one - scaled * mean_two)


def taps_last(padded, kernel, row_count, col_count, flipped):
    summed = jnp.zeros(padded.shape[:-3] + (row_count, col_count, padded.shape[-1]), jnp.float32)
    for tap_index in range(49):
        row_off = tap_index // 7
        col_off = tap_index % 7
        if flipped:
            row_off = 6 - row_off
            col_off = 6 - col_off
        summed = (
            summed
            + padded[..., row_off : row_off + row_count, col_off : col_off + col_count, :]
            * kernel[tap_index]
        )
    return summed


def contract_last(left_side, right_side):
    return lax.dot_general(
        left_side, right_side, (((1,), (1,)), ((), ())), preferred_element_type=jnp.float32
    )


def dense_forward(normed, weights, up_bias, down_bias):
    width = normed.shape[1]
    pre_acts = []
    branch = down_bias
    for part, part_bias in zip(weights, up_bias):
        pre_act = contract_last(normed, part[:, :width]) + part_bias
        hidden = gelu_exact(pre_act).astype(jnp.bfloat16)
        branch = branch + jnp.dot(hidden, part[:, width:], preferred_element_type=jnp.float32)
        pre_acts.append(pre_act)
    return (branch, pre_acts)


def dense_backward(d_branch, pre_acts, weights):
    width = d_branch.shape[1]
    total = 0.0
    for part, pre_act in zip(weights, pre_acts):
        d_hidden = contract_last(d_branch, part[:, width:])
        d_pre = (d_hidden * gelu_slope(pre_act)).astype(jnp.bfloat16)
        total = total + jnp.dot(d_pre, part[:, :width], preferred_element_type=jnp.float32)
    return total


def with_rims(tile_values):
    return with_halo(tile_values, (("row", 1), ("col", 2)), 3)


def on_device(
    images,
    kernel_one,
    gain_one,
    shift_one,
    up_one,
    up_bias_one,
    down_one,
    down_bias_one,
    scale_one,
    gain_mid,
    shift_mid,
    merge_weight,
    merge_bias,
    kernel_two,
    gain_two,
    shift_two,
    up_two,
    up_bias_two,
    down_two,
    down_bias_two,
    scale_two,
    grad_out,
):
    micro_count, tile_rows, tile_cols, width_one = images.shape
    width_two = merge_weight.shape[1]
    half_rows = tile_rows // 2
    half_cols = tile_cols // 2
    rows_one = micro_count * tile_rows * tile_cols
    rows_two = micro_count * half_rows * half_cols

    swap = [(0, 1), (1, 0)]
    side = lax.axis_index("sec")

    def both_halves(own):
        return (own, lax.ppermute(own, "sec", swap))

    def bias_halves(bias):
        halves = bias.reshape(2, -1)
        return (
            lax.dynamic_index_in_dim(halves, side, 0, keepdims=False),
            lax.dynamic_index_in_dim(halves, 1 - side, 0, keepdims=False),
        )

    share_one = up_one.shape[1]
    share_two = up_two.shape[1]
    packed = jnp.concatenate(
        [up_two.T, down_two.T, jnp.concatenate([up_one.T, down_one.T], axis=1)], axis=0
    )
    column = lax.all_gather(packed, "col", axis=0, tiled=False)
    part_one = column[:, 2 * share_two :].reshape(-1, 2 * width_one)
    part_two = jnp.concatenate(
        [
            column[:, :share_two].reshape(-1, width_two),
            column[:, share_two : 2 * share_two].reshape(-1, width_two),
        ],
        axis=1,
    )
    own_one = lax.all_gather(part_one, "row", axis=0, tiled=True)
    own_two = lax.all_gather(part_two, "row", axis=0, tiled=True)
    pair_one = both_halves(own_one)
    pair_two = both_halves(own_two)
    bias_one = bias_halves(up_bias_one)
    bias_two = bias_halves(up_bias_two)

    padded_one = with_rims(images).astype(jnp.float32)
    conv_one = taps_last(padded_one, kernel_one, tile_rows, tile_cols, False).reshape(
        rows_one, width_one
    )
    scaled_one, inv_one, normed_one = norm_forward(conv_one, gain_one, shift_one)
    normed_one = normed_one.astype(jnp.bfloat16)
    branch_one, pre_one = dense_forward(normed_one, pair_one, bias_one, down_bias_one)
    section_out = (
        images.reshape(rows_one, width_one).astype(jnp.float32) + scale_one * branch_one
    ).astype(jnp.bfloat16)
    scaled_mid, inv_mid, normed_mid = norm_forward(
        section_out.astype(jnp.float32), gain_mid, shift_mid
    )
    patches = normed_mid.astype(jnp.bfloat16).reshape(
        micro_count, half_rows, 2, half_cols, 2, width_one
    )
    patches = patches.transpose(0, 1, 3, 2, 4, 5).reshape(rows_two, 4 * width_one)
    merged = (
        jnp.dot(patches, merge_weight, preferred_element_type=jnp.float32) + merge_bias
    ).astype(jnp.bfloat16)
    merged_tile = merged.reshape(micro_count, half_rows, half_cols, width_two)
    padded_two = with_rims(merged_tile).astype(jnp.float32)
    conv_two = (
        taps_last(padded_two, kernel_two, half_rows, half_cols, False)
        .reshape(rows_two, width_two)
        .astype(jnp.bfloat16)
    )
    scaled_two, inv_two, normed_two = norm_forward(
        conv_two.astype(jnp.float32), gain_two, shift_two
    )
    normed_two = normed_two.astype(jnp.bfloat16)
    branch_two, pre_two = dense_forward(normed_two, pair_two, bias_two, down_bias_two)
    features = (merged.astype(jnp.float32) + scale_two * branch_two).astype(jnp.bfloat16)
    grad_rows = grad_out.reshape(rows_two, width_two)
    d_branch_two = (grad_rows.astype(jnp.float32) * scale_two).astype(jnp.bfloat16)
    d_normed_two = dense_backward(d_branch_two, pre_two, pair_two)
    d_conv_two = norm_backward(d_normed_two, scaled_two, inv_two, gain_two).astype(jnp.bfloat16)
    back_tile = d_conv_two.reshape(micro_count, half_rows, half_cols, width_two)
    padded_back = with_rims(back_tile).astype(jnp.float32)
    d_taps = (
        taps_last(padded_back, kernel_two, half_rows, half_cols, True)
        .reshape(rows_two, width_two)
        .astype(jnp.bfloat16)
    )
    d_taps = lax.optimization_barrier(d_taps).astype(jnp.float32)
    d_merged = (d_taps + grad_rows.astype(jnp.float32)).astype(jnp.bfloat16)
    d_patches = contract_last(d_merged, merge_weight)
    d_normed_mid = d_patches.reshape(micro_count, half_rows, half_cols, 2, 2, width_one)
    d_normed_mid = d_normed_mid.transpose(0, 1, 3, 2, 4, 5).reshape(rows_one, width_one)
    upstream_one = norm_backward(d_normed_mid, scaled_mid, inv_mid, gain_mid)
    d_branch_one = (upstream_one * scale_one).astype(jnp.bfloat16)
    d_normed_one = dense_backward(d_branch_one, pre_one, pair_one)
    d_conv_one = norm_backward(d_normed_one, scaled_one, inv_one, gain_one).astype(jnp.bfloat16)
    d_conv_one = d_conv_one.reshape(micro_count, tile_rows, tile_cols, width_one)
    padded_grad = with_rims(d_conv_one).astype(jnp.float32)
    back_one = taps_last(padded_grad, kernel_one, tile_rows, tile_cols, True).reshape(
        rows_one, width_one
    )
    input_grad = (back_one + upstream_one).astype(jnp.bfloat16).reshape(images.shape)
    return (features.reshape(micro_count, half_rows, half_cols, width_two), input_grad)


def solution(mesh):
    in_specs = (
        P("sec", "row", "col", None),
        P(),
        P(),
        P(),
        P(None, ("sec", "row", "col")),
        P(),
        P(None, ("sec", "row", "col")),
        P(),
        P(),
        P(),
        P(),
        P(),
        P(),
        P(),
        P(),
        P(),
        P(None, ("sec", "row", "col")),
        P(),
        P(None, ("sec", "row", "col")),
        P(),
        P(),
        P("sec", "row", "col", None),
    )
    out_specs = (P("sec", "row", "col", None), P("sec", "row", "col", None))
    return jax.shard_map(
        on_device, mesh=mesh, in_specs=in_specs, out_specs=out_specs, check_vma=False
    )
```

time: 619 us -> 295 us (0.48); the launches traced: 609 us -> 293 us
  waiting for transfers between devices: 325 us -> 88.6 us
  local copies, waits for them, and re-layouts: 92.8 us -> 28.2 us
  blocking collectives: 65.6 us -> 29 us
  starting transfers between devices: 38.6 us -> 51.6 us
  matrix products: 31.2 us -> 41.2 us
    all_gather x4 -> x2, waiting for transfers between devices: 309 us -> 70.4 us  [the longest x1 55.5 us: on_device(): own_two = lax.all_gather(part_two, 'row', axis=0, tiled=True)]
    all_to_all x3 -> x0, blocking collectives: 65.6 us -> none  [regroup(): lax.all_to_all(blocks, ('row', 'col'), split_axis=0, concat_axis=0, tiled...]
    all_gather x0 -> x1, blocking collectives: none -> 29 us  [on_device(): column = lax.all_gather(packed, 'col', axis=0, tiled=False)]
    convert_element_type x10 -> x0, local copies, waits for them, and re-layouts: 25 us -> none  [the longest x3 9.92 us: on_device(): padded_two = jnp.pad(picture.astype(jnp.float32), frame_pads)]
    unnamed x214 -> x396, local copies, waits for them, and re-layouts: 25.2 us -> 3.28 us
    dot_general x2 -> x8, matrix products: 7.65 us -> 27.4 us  [the longest x4 18.6 us: dense_backward(): jnp.dot(d_pre, part[:, :width], preferred_element_type=jnp.float32)]
    reshape x9 -> x5, local copies, waits for them, and re-layouts: 19.9 us -> 1.68 us  [the longest x1 0.96 us: on_device(): column[:, :share_two].reshape(-1, width_two)]
    ppermute x4 -> x8, starting transfers between devices: 11.4 us -> 27.4 us  [with_halo(): lax.ppermute(lax.slice_in_dim(block, 0, width, axis=dim), axis, backward)]
  transfers between devices with their start and end apart: 13 -> 20, of which waited for: 7 -> 13; matrix products, arithmetic and copies ran while one was open for 14% -> 18% of each run, Pallas kernels for 0% -> 0%
where the time goes in v1:
time: 295 us; the launch traced here: 293 us
  waiting for transfers between devices  88.6 us (30%)
  starting transfers between devices  51.6 us (17%)
  matrix products  41.2 us (14%)
  other arithmetic  36.6 us (12%)
  blocking collectives  29 us (10%)
  local copies, waits for them, and re-layouts  28.2 us (10%)
  between operations  17.3 us (6%)
    all_gather x1, waiting for transfers between devices, on_device(): own_two = lax.all_gather(part_two, 'row', axis=0, tiled=True)  55.5 us
    all_gather x1, blocking collectives, on_device(): column = lax.all_gather(packed, 'col', axis=0, tiled=False)  29 us
    ppermute x8, starting transfers between devices, with_halo(): lax.ppermute(lax.slice_in_dim(block, 0, width, axis=dim), axis, backward)  27.4 us
    ppermute x8, starting transfers between devices, with_halo(): lax.ppermute(lax.slice_in_dim(block, block.shape[dim] - width, None, axis...  24.1 us
    dot_general x4, matrix products, dense_backward(): jnp.dot(d_pre, part[:, :width], preferred_element_type=jnp.float32)  18.6 us
    ppermute x8, waiting for transfers between devices, with_halo(): lax.ppermute(lax.slice_in_dim(block, 0, width, axis=dim), axis, backward)  15.4 us
    all_gather x1, waiting for transfers between devices, on_device(): own_one = lax.all_gather(part_one, 'row', axis=0, tiled=True)  14.9 us
    dot_general x5, matrix products, contract_last(): lax.dot_general(left_side, right_side, (((1,), (1,)), ((), ())), preferre...  12.3 us
  transfers between devices with their start and end apart: 20, of which 13 were waited for; matrix products, arithmetic and copies ran while one was open for 18% of the time, Pallas kernels for 0%

profile of v1, /device:TPU:2, one launch (start us, length us, event | category | flops | bytes accessed | tf_op | source)
XLA Modules:
  0.0 292.5 jit_solution(5238632665274665715)
XLA Ops:
  8.2 29.0 %all-gather.1 = bf16[8,30,768]{2,1,0:T(8,128)(2,1)S(1)} all-gather(bf16[1,30,768]{2,1,0:T(8,128)(2,1)S(1)} %maximum_bitcast_fusion), channel_id=2, replica_groups=mesh['sec'=2,'row'=16,'col'=8] {'col'}, dimensions={0}, use_global_device_ids=true | all-gather | bytes 414720 | tf_op jit(solution)/shard_map/all_gather | solution.py:144
  40.5 4.9 %collective-permute-start.1 = (bf16[1,3,32,384]{3,2,1,0:T(8,128)(2,1)S(1)}, bf16[1,3,32,384]{3,2,1,0:T(8,128)(2,1)S(1)}, u32[]{:S(2)}, u32[]{:S(2)}) collective-permute-start(bf16[1,3,32,384]{3,2,1,0:T(8,128)(2,1)S(1)} %get-tuple-element.118), channel_id=1, source_target_pairs={{8,0},{16,8},{24,16},{32,24},{40,32},{48,40},{56,48},{64,56},{72,6... | collective-permute-start | bytes 221192 | tf_op jit(solution)/shard_map/ppermute | solution.py:17
  63.4 6.5 %fusion.322 = (f32[16,32]{1,0:T(8,128)S(1)}, f32[1,16,32,384]{3,2,1,0:T(8,128)S(1)}) fusion(f32[384]{0:T(512)} %get-tuple-element.102, f32[1,22,38,384]{3,2,1,0:T(8,128)S(1)} %maximum_convert_fusion, f32[384]{0:T(512)} %get-tuple-element.103, f32[384]{0:T(512)S(1)} %get-tuple-element.56, f32[384]{0:T(512)S(1)} %get-tuple-element.57, ...), kind=kLoop, calls=%fused_computation.666 | loop fusion | flops 19267072 | bytes 39398912 | tf_op jit(solution)/shard_map/reduce_sum | solution.py:34
  70.1 14.9 %all-gather.5.cloned.1.call-done = bf16[768,768]{1,0:T(8,128)(2,1)} async-done(((bf16[48,768]{1,0:T(8,128)(2,1)}), bf16[768,768]{1,0:T(8,128)(2,1)}) %all-gather.5.cloned.1.call-update) | async-done | bytes 1179664 | tf_op jit(solution)/shard_map/all_gather | solution.py:153
  91.3 55.5 %all-gather.7.cloned.1.call-done = bf16[1536,1536]{1,0:T(8,128)(2,1)} async-done(((bf16[96,1536]{1,0:T(8,128)(2,1)}), bf16[1536,1536]{1,0:T(8,128)(2,1)}) %all-gather.7.cloned.1.call-update) | async-done | bytes 4718608 | tf_op jit(solution)/shard_map/all_gather | solution.py:154
  160.8 5.8 %collective-permute-start.6 = (bf16[1,3,16,768]{3,2,1,0:T(8,128)(2,1)S(1)}, bf16[1,3,16,768]{3,2,1,0:T(8,128)(2,1)S(1)}, u32[]{:S(2)}, u32[]{:S(2)}) collective-permute-start(bf16[1,3,16,768]{3,2,1,0:T(8,128)(2,1)S(1)} %get-tuple-element.129), channel_id=1, source_target_pairs={{8,0},{16,8},{24,16},{32,24},{40,32},{48,40},{56,48},{64,56},{72,6... | collective-permute-start | bytes 221192 | tf_op jit(solution)/shard_map/ppermute | solution.py:17
  168.7 3.5 %collective-permute-start.7 = (bf16[1,14,3,768]{3,2,1,0:T(4,128)(2,1)S(1)}, bf16[1,14,3,768]{3,2,1,0:T(4,128)(2,1)S(1)}, u32[]{:S(2)}, u32[]{:S(2)}) collective-permute-start(bf16[1,14,3,768]{3,2,1,0:T(4,128)(2,1)S(1)} %get-tuple-element.124), channel_id=1, source_target_pairs={{0,1},{1,2},{2,3},{3,4},{4,5},{5,6},{6,7},{8,9},{9,10},{10,11},{11... | collective-permute-start | bytes 193544 | tf_op jit(solution)/shard_map/ppermute | solution.py:14
  174.2 4.3 %collective-permute-done.8 = bf16[1,14,3,768]{3,2,1,0:T(4,128)(2,1)S(1)} collective-permute-done((bf16[1,14,3,768]{3,2,1,0:T(4,128)(2,1)S(1)}, bf16[1,14,3,768]{3,2,1,0:T(4,128)(2,1)S(1)}, u32[]{:S(2)}, u32[]{:S(2)}) %collective-permute-start.8) | collective-permute-done | bytes 64544 | tf_op jit(solution)/shard_map/ppermute | solution.py:17
  178.9 4.1 %convert_reduce_fusion = (f32[8,16]{1,0:T(8,128)S(1)}, bf16[1,8,16,768]{3,2,1,0:T(8,128)(2,1)S(1)}) fusion(f32[768]{0:T(1024)S(1)} %get-tuple-element.53, f32[1,14,22,768]{3,2,1,0:T(8,128)S(1)} %maximum_convert_fusion.2, f32[768]{0:T(1024)S(1)} %get-tuple-element.54, f32[768]{0:T(1024)S(1)} %get-tuple-element.7, f32[768]{0:T(1024)S(1)} %get-tuple-element.8, ...), kind=kLoop, calls=%fused_computation.518 | loop fusion | flops 9830272 | bytes 19615232 | tf_op jit(solution)/shard_map/reduce_sum | solution.py:34
  186.3 3.5 %convolution_add_fusion.1 = f32[128,1536]{1,0:T(8,128)} fusion(bf16[128,768]{1,0:T(8,128)(2,1)S(1)} %add_convert_fusion.2, bf16[1536,1536]{1,0:T(8,128)(2,1)} %all-gather.7.cloned.1.call-done, f32[1536]{0:T(1024)} %get-tuple-element.105), kind=kOutput, calls=%fused_computation.3 | convolution fusion | flops 302186496 | bytes 3350528 | tf_op jit(solution)/shard_map/dot_general | solution.py:64
  189.8 4.7 %fusion.11 = f32[128,768]{1,0:T(8,128)} fusion(bf16[1536,1536]{1,0:T(8,128)(2,1)} %all-gather.7.cloned.1.call-done, bf16[128,768]{1,0:T(8,128)(2,1)} %fusion.192, f32[128,1536]{1,0:T(8,128)} %convolution_add_fusion.1), kind=kOutput, calls=%fused_computation.17 | convolution fusion | flops 605945856 | bytes 6094848 | tf_op jit(solution)/shard_map/dot_general | solution.py:87
  194.5 3.5 %convolution_add_fusion = f32[128,1536]{1,0:T(8,128)} fusion(bf16[128,768]{1,0:T(8,128)(2,1)} %copy-done.13, bf16[1536,1536]{1,0:T(8,128)(2,1)} %collective-permute-done.9, f32[1536]{0:T(1024)} %get-tuple-element.104), kind=kOutput, calls=%fused_computation.2 | convolution fusion | flops 302186496 | bytes 3350528 | tf_op jit(solution)/shard_map/dot_general | solution.py:64
  198.0 5.3 %fusion.320 = (f32[128]{0:T(128)}, f32[128]{0:T(128)}, f32[128,768]{1,0:T(8,128)}) fusion(f32[128]{0:T(128)} %rsqrt.34, f32[128]{0:T(128)S(1)} %copy-done.186, bf16[1,8,16,768]{3,2,1,0:T(8,128)(2,1)S(1)} %get-tuple-element.109, f32[768]{0:T(1024)} %param.36, f32[128,768]{1,0:T(8,128)} %fusion.11, bf16[1536,1536]{1,0:T(8,128)(2,1)} %collective-permute-done.9, ...), kind=kOutput, calls=%fused_computation.665 | convolution fusion | flops 606732032 | bytes 6689792 | tf_op jit(solution)/shard_map/dot_general | solution.py:87
  207.4 6.4 %collective-permute-start.11 = (bf16[1,3,16,768]{3,2,1,0:T(8,128)(2,1)S(1)}, bf16[1,3,16,768]{3,2,1,0:T(8,128)(2,1)S(1)}, u32[]{:S(2)}, u32[]{:S(2)}) collective-permute-start(bf16[1,3,16,768]{3,2,1,0:T(8,128)(2,1)S(1)} %get-tuple-element.127), channel_id=1, source_target_pairs={{8,0},{16,8},{24,16},{32,24},{40,32},{48,40},{56,48},{64,56},{72,6... | collective-permute-start | bytes 221192 | tf_op jit(solution)/shard_map/ppermute | solution.py:17
  215.9 3.5 %collective-permute-start.12 = (bf16[1,14,3,768]{3,2,1,0:T(4,128)(2,1)S(1)}, bf16[1,14,3,768]{3,2,1,0:T(4,128)(2,1)S(1)}, u32[]{:S(2)}, u32[]{:S(2)}) collective-permute-start(bf16[1,14,3,768]{3,2,1,0:T(4,128)(2,1)S(1)} %get-tuple-element.122), channel_id=1, source_target_pairs={{0,1},{1,2},{2,3},{3,4},{4,5},{5,6},{6,7},{8,9},{9,10},{10,11},{11... | collective-permute-start | bytes 193544 | tf_op jit(solution)/shard_map/ppermute | solution.py:14
  221.4 4.6 %collective-permute-done.13 = bf16[1,14,3,768]{3,2,1,0:T(4,128)(2,1)S(1)} collective-permute-done((bf16[1,14,3,768]{3,2,1,0:T(4,128)(2,1)S(1)}, bf16[1,14,3,768]{3,2,1,0:T(4,128)(2,1)S(1)}, u32[]{:S(2)}, u32[]{:S(2)}) %collective-permute-start.13) | collective-permute-done | bytes 64544 | tf_op jit(solution)/shard_map/ppermute | solution.py:17
  226.6 3.6 %fusion.195 = bf16[1,8,16,768]{3,2,1,0:T(8,128)(2,1)S(1)} fusion(f32[1,14,22,768]{3,2,1,0:T(8,128)S(1)} %maximum_convert_fusion.3, f32[768]{0:T(1024)} %copy-done.99, f32[768]{0:T(1024)} %copy-done.100, f32[768]{0:T(1024)S(1)} %get-tuple-element.7, f32[768]{0:T(1024)S(1)} %copy-done.16, f32[768]{0:T(1024)S(1)} %copy-done.18, f32[768]{0:T(1024)S(1)} %copy-done.20, ...), kind=kLoop, calls=%fused_computation.309 | loop fusion | flops 9633792 | bytes 19614720 | tf_op jit(solution)/shard_map/convert_element_type | solution.py:202
  245.7 4.2 %fusion.31 = f32[512,384]{1,0:T(8,128)} fusion(f32[512,768]{1,0:T(8,128)} %copy-done.8, bf16[768,768]{1,0:T(8,128)(2,1)} %all-gather.5.cloned.1.call-done, f32[512,384]{1,0:T(8,128)} %subtract_multiply_fusion, f32[384]{0:T(512)S(1)} %copy-done.192), kind=kOutput, calls=%fused_computation.39 | convolution fusion | flops 608305152 | bytes 4326912 | tf_op jit(solution)/shard_map/dot_general | solution.py:87
  249.9 4.4 %fusion.319 = (f32[512]{0:T(512)S(1)}, f32[512]{0:T(512)S(1)}, f32[512,384]{1,0:T(8,128)}) fusion(f32[512]{0:T(512)S(1)} %copy-done.183, f32[512]{0:T(512)S(1)} %copy-done.182, f32[1,16,32,384]{3,2,1,0:T(8,128)S(1)} %copy-done.2, f32[384]{0:T(512)S(1)} %copy-done.190, f32[512,384]{1,0:T(8,128)} %fusion.31, bf16[768,768]{1,0:T(8,128)(2,1)} %collective-permute-done.4, ...), kind=kOutput, calls=%fused_computation.664 | convolution fusion | flops 609680384 | bytes 5909504 | tf_op jit(solution)/shard_map/dot_general | solution.py:87
  255.9 3.7 %collective-permute-start.14 = (bf16[1,3,32,384]{3,2,1,0:T(8,128)(2,1)S(1)}, bf16[1,3,32,384]{3,2,1,0:T(8,128)(2,1)S(1)}, u32[]{:S(2)}, u32[]{:S(2)}) collective-permute-start(bf16[1,3,32,384]{3,2,1,0:T(8,128)(2,1)S(1)} %get-tuple-element.116), channel_id=1, source_target_pairs={{0,8},{8,16},{16,24},{24,32},{32,40},{40,48},{48,56},{56,64},{64,7... | collective-permute-start | bytes 221192 | tf_op jit(solution)/shard_map/ppermute | solution.py:14
  259.6 4.8 %collective-permute-start.15 = (bf16[1,3,32,384]{3,2,1,0:T(8,128)(2,1)S(1)}, bf16[1,3,32,384]{3,2,1,0:T(8,128)(2,1)S(1)}, u32[]{:S(2)}, u32[]{:S(2)}) collective-permute-start(bf16[1,3,32,384]{3,2,1,0:T(8,128)(2,1)S(1)} %get-tuple-element.117), channel_id=1, source_target_pairs={{8,0},{16,8},{24,16},{32,24},{40,32},{48,40},{56,48},{64,56},{72,6... | collective-permute-start | bytes 221192 | tf_op jit(solution)/shard_map/ppermute | solution.py:17
  266.6 5.1 %collective-permute-start.16 = (bf16[1,22,3,384]{3,2,1,0:T(4,128)(2,1)S(1)}, bf16[1,22,3,384]{3,2,1,0:T(4,128)(2,1)S(1)}, u32[]{:S(2)}, u32[]{:S(2)}) collective-permute-start(bf16[1,22,3,384]{3,2,1,0:T(4,128)(2,1)S(1)} %get-tuple-element.112), channel_id=1, source_target_pairs={{0,1},{1,2},{2,3},{3,4},{4,5},{5,6},{6,7},{8,9},{9,10},{10,11},{11... | collective-permute-start | bytes 152072 | tf_op jit(solution)/shard_map/ppermute | solution.py:14
  273.1 2.9 fusion.60
  278.6 6.3 %fusion.74 = f32[1,16,32,384]{3,2,1,0:T(8,128)S(1)} fusion(f32[1,22,38,384]{3,2,1,0:T(8,128)S(1)} %maximum_convert_fusion.1, f32[384]{0:T(512)} %get-tuple-element.102, f32[384]{0:T(512)} %get-tuple-element.103, f32[384]{0:T(512)S(1)} %copy-done.108, f32[384]{0:T(512)S(1)} %copy-done.110, f32[384]{0:T(512)S(1)} %copy-done.112, f32[384]{0:T(512)S(1)} %copy-done.114, ...), kind=kLoop, calls=%fused_computation.68 | loop fusion | flops 19070976 | bytes 39396864 | tf_op jit(solution)/shard_map/add | solution.py:56
  (498 shorter events, 80.3 us)
Async XLA Ops:
  7.2 149.8 %copy-start = (bf16[1536,768]{1,0:T(8,128)(2,1)S(1)}, bf16[1536,768]{1,0:T(8,128)(2,1)}, u32[]{:S(2)}) copy-start(bf16[1536,768]{1,0:T(8,128)(2,1)} %param.33) | copy-start | bytes 7077892
  7.2 77.8 %all-gather.5.cloned.1.call-start = ((), (), s32[]{:S(2)}) async-start(), calls=%async_computation | async-start | bytes 1253376 | tf_op jit(solution)/shard_map/all_gather | solution.py:153
  8.2 32.3 %copy-start.6 = (bf16[1,16,32,384]{3,2,1,0:T(8,128)(2,1)S(1)}, bf16[1,16,32,384]{3,2,1,0:T(8,128)(2,1)}, u32[]{:S(2)}) copy-start(bf16[1,16,32,384]{3,2,1,0:T(8,128)(2,1)} %param.22) | copy-start | bytes 1179652
  37.9 108.9 %all-gather.7.cloned.1.call-start = ((), (), s32[]{:S(2)}) async-start(), calls=%async_computation.1 | async-start | bytes 5013504 | tf_op jit(solution)/shard_map/all_gather | solution.py:154
  40.5 13.6 %collective-permute-start.1 = (bf16[1,3,32,384]{3,2,1,0:T(8,128)(2,1)S(1)}, bf16[1,3,32,384]{3,2,1,0:T(8,128)(2,1)S(1)}, u32[]{:S(2)}, u32[]{:S(2)}) collective-permute-start(bf16[1,3,32,384]{3,2,1,0:T(8,128)(2,1)S(1)} %get-tuple-element.118), channel_id=1, source_target_pairs={{8,0},{16,8},{24,16},{32,24},{40,32},{48,40},{56,48},{64,56},{72,6... | collective-permute-start | bytes 221192 | tf_op jit(solution)/shard_map/ppermute | solution.py:17
  45.4 8.6 %collective-permute-start = (bf16[1,3,32,384]{3,2,1,0:T(8,128)(2,1)S(1)}, bf16[1,3,32,384]{3,2,1,0:T(8,128)(2,1)S(1)}, u32[]{:S(2)}, u32[]{:S(2)}) collective-permute-start(bf16[1,3,32,384]{3,2,1,0:T(8,128)(2,1)S(1)} %get-tuple-element.119), channel_id=1, source_target_pairs={{0,8},{8,16},{16,24},{24,32},{32,40},{40,48},{48,56},{56,64},{64,7... | collective-permute-start | bytes 221192 | tf_op jit(solution)/shard_map/ppermute | solution.py:14
  50.8 127.9 %copy-start.15 = (f32[768]{0:T(1024)}, f32[768]{0:T(1024)S(1)}, u32[]{:S(2)}) copy-start(f32[768]{0:T(1024)S(1)} %get-tuple-element.8) | copy-start | bytes 9220
  54.2 6.6 %collective-permute-start.2 = (bf16[1,22,3,384]{3,2,1,0:T(4,128)(2,1)S(1)}, bf16[1,22,3,384]{3,2,1,0:T(4,128)(2,1)S(1)}, u32[]{:S(2)}, u32[]{:S(2)}) collective-permute-start(bf16[1,22,3,384]{3,2,1,0:T(4,128)(2,1)S(1)} %get-tuple-element.114), channel_id=1, source_target_pairs={{0,1},{1,2},{2,3},{3,4},{4,5},{5,6},{6,7},{8,9},{9,10},{10,11},{11... | collective-permute-start | bytes 152072 | tf_op jit(solution)/shard_map/ppermute | solution.py:14
  56.7 6.2 %collective-permute-start.3 = (bf16[1,22,3,384]{3,2,1,0:T(4,128)(2,1)S(1)}, bf16[1,22,3,384]{3,2,1,0:T(4,128)(2,1)S(1)}, u32[]{:S(2)}, u32[]{:S(2)}) collective-permute-start(bf16[1,22,3,384]{3,2,1,0:T(4,128)(2,1)S(1)} %get-tuple-element.115), channel_id=1, source_target_pairs={{1,0},{2,1},{3,2},{4,3},{5,4},{6,5},{7,6},{9,8},{10,9},{11,10},{12... | collective-permute-start | bytes 152072 | tf_op jit(solution)/shard_map/ppermute | solution.py:17
  85.0 61.8 %collective-permute-start.4 = (bf16[768,768]{1,0:T(8,128)(2,1)}, bf16[768,768]{1,0:T(8,128)(2,1)}, u32[]{:S(2)}, u32[]{:S(2)}) collective-permute-start(bf16[768,768]{1,0:T(8,128)(2,1)} %all-gather.5.cloned.1.call-done), channel_id=1, source_target_pairs={{0,128},{128,0},{1,129},{129,1},{2,130},{130,2},{3,131},{131,3},{4... | collective-permute-start | bytes 3538952 | tf_op jit(solution)/shard_map/ppermute | solution.py:130
  91.3 57.3 %copy-start.191 = (f32[384]{0:T(512)S(1)}, f32[384]{0:T(512)}, u32[]{:S(2)}) copy-start(f32[384]{0:T(512)} %param.30) | copy-start | bytes 4612
  146.8 47.7 %collective-permute-start.9 = (bf16[1536,1536]{1,0:T(8,128)(2,1)}, bf16[1536,1536]{1,0:T(8,128)(2,1)}, u32[]{:S(2)}, u32[]{:S(2)}) collective-permute-start(bf16[1536,1536]{1,0:T(8,128)(2,1)} %all-gather.7.cloned.1.call-done), channel_id=1, source_target_pairs={{0,128},{128,0},{1,129},{129,1},{2,130},{130,2},{3,131},{131,3},{4... | collective-permute-start | bytes 14155784 | tf_op jit(solution)/shard_map/ppermute | solution.py:130
  158.7 8.6 %collective-permute-start.5 = (bf16[1,3,16,768]{3,2,1,0:T(8,128)(2,1)S(1)}, bf16[1,3,16,768]{3,2,1,0:T(8,128)(2,1)S(1)}, u32[]{:S(2)}, u32[]{:S(2)}) collective-permute-start(bf16[1,3,16,768]{3,2,1,0:T(8,128)(2,1)S(1)} %get-tuple-element.128), channel_id=1, source_target_pairs={{0,8},{8,16},{16,24},{24,32},{32,40},{40,48},{48,56},{56,64},{64,7... | collective-permute-start | bytes 221192 | tf_op jit(solution)/shard_map/ppermute | solution.py:14
  160.8 7.8 %collective-permute-start.6 = (bf16[1,3,16,768]{3,2,1,0:T(8,128)(2,1)S(1)}, bf16[1,3,16,768]{3,2,1,0:T(8,128)(2,1)S(1)}, u32[]{:S(2)}, u32[]{:S(2)}) collective-permute-start(bf16[1,3,16,768]{3,2,1,0:T(8,128)(2,1)S(1)} %get-tuple-element.129), channel_id=1, source_target_pairs={{8,0},{16,8},{24,16},{32,24},{40,32},{48,40},{56,48},{64,56},{72,6... | collective-permute-start | bytes 221192 | tf_op jit(solution)/shard_map/ppermute | solution.py:17
  168.7 5.5 %collective-permute-start.7 = (bf16[1,14,3,768]{3,2,1,0:T(4,128)(2,1)S(1)}, bf16[1,14,3,768]{3,2,1,0:T(4,128)(2,1)S(1)}, u32[]{:S(2)}, u32[]{:S(2)}) collective-permute-start(bf16[1,14,3,768]{3,2,1,0:T(4,128)(2,1)S(1)} %get-tuple-element.124), channel_id=1, source_target_pairs={{0,1},{1,2},{2,3},{3,4},{4,5},{5,6},{6,7},{8,9},{9,10},{10,11},{11... | collective-permute-start | bytes 193544 | tf_op jit(solution)/shard_map/ppermute | solution.py:14
  172.1 6.4 %collective-permute-start.8 = (bf16[1,14,3,768]{3,2,1,0:T(4,128)(2,1)S(1)}, bf16[1,14,3,768]{3,2,1,0:T(4,128)(2,1)S(1)}, u32[]{:S(2)}, u32[]{:S(2)}) collective-permute-start(bf16[1,14,3,768]{3,2,1,0:T(4,128)(2,1)S(1)} %get-tuple-element.125), channel_id=1, source_target_pairs={{1,0},{2,1},{3,2},{4,3},{5,4},{6,5},{7,6},{9,8},{10,9},{11,10},{12... | collective-permute-start | bytes 193544 | tf_op jit(solution)/shard_map/ppermute | solution.py:17
  205.5 8.7 %collective-permute-start.10 = (bf16[1,3,16,768]{3,2,1,0:T(8,128)(2,1)S(1)}, bf16[1,3,16,768]{3,2,1,0:T(8,128)(2,1)S(1)}, u32[]{:S(2)}, u32[]{:S(2)}) collective-permute-start(bf16[1,3,16,768]{3,2,1,0:T(8,128)(2,1)S(1)} %get-tuple-element.126), channel_id=1, source_target_pairs={{0,8},{8,16},{16,24},{24,32},{32,40},{40,48},{48,56},{56,64},{64,7... | collective-permute-start | bytes 221192 | tf_op jit(solution)/shard_map/ppermute | solution.py:14
  207.4 8.4 %collective-permute-start.11 = (bf16[1,3,16,768]{3,2,1,0:T(8,128)(2,1)S(1)}, bf16[1,3,16,768]{3,2,1,0:T(8,128)(2,1)S(1)}, u32[]{:S(2)}, u32[]{:S(2)}) collective-permute-start(bf16[1,3,16,768]{3,2,1,0:T(8,128)(2,1)S(1)} %get-tuple-element.127), channel_id=1, source_target_pairs={{8,0},{16,8},{24,16},{32,24},{40,32},{48,40},{56,48},{64,56},{72,6... | collective-permute-start | bytes 221192 | tf_op jit(solution)/shard_map/ppermute | solution.py:17
  215.9 5.5 %collective-permute-start.12 = (bf16[1,14,3,768]{3,2,1,0:T(4,128)(2,1)S(1)}, bf16[1,14,3,768]{3,2,1,0:T(4,128)(2,1)S(1)}, u32[]{:S(2)}, u32[]{:S(2)}) collective-permute-start(bf16[1,14,3,768]{3,2,1,0:T(4,128)(2,1)S(1)} %get-tuple-element.122), channel_id=1, source_target_pairs={{0,1},{1,2},{2,3},{3,4},{4,5},{5,6},{6,7},{8,9},{9,10},{10,11},{11... | collective-permute-start | bytes 193544 | tf_op jit(solution)/shard_map/ppermute | solution.py:14
  219.3 6.7 %collective-permute-start.13 = (bf16[1,14,3,768]{3,2,1,0:T(4,128)(2,1)S(1)}, bf16[1,14,3,768]{3,2,1,0:T(4,128)(2,1)S(1)}, u32[]{:S(2)}, u32[]{:S(2)}) collective-permute-start(bf16[1,14,3,768]{3,2,1,0:T(4,128)(2,1)S(1)} %get-tuple-element.123), channel_id=1, source_target_pairs={{1,0},{2,1},{3,2},{4,3},{5,4},{6,5},{7,6},{9,8},{10,9},{11,10},{12... | collective-permute-start | bytes 193544 | tf_op jit(solution)/shard_map/ppermute | solution.py:17
  255.9 10.7 %collective-permute-start.14 = (bf16[1,3,32,384]{3,2,1,0:T(8,128)(2,1)S(1)}, bf16[1,3,32,384]{3,2,1,0:T(8,128)(2,1)S(1)}, u32[]{:S(2)}, u32[]{:S(2)}) collective-permute-start(bf16[1,3,32,384]{3,2,1,0:T(8,128)(2,1)S(1)} %get-tuple-element.116), channel_id=1, source_target_pairs={{0,8},{8,16},{16,24},{24,32},{32,40},{40,48},{48,56},{56,64},{64,7... | collective-permute-start | bytes 221192 | tf_op jit(solution)/shard_map/ppermute | solution.py:14
  259.6 7.0 %collective-permute-start.15 = (bf16[1,3,32,384]{3,2,1,0:T(8,128)(2,1)S(1)}, bf16[1,3,32,384]{3,2,1,0:T(8,128)(2,1)S(1)}, u32[]{:S(2)}, u32[]{:S(2)}) collective-permute-start(bf16[1,3,32,384]{3,2,1,0:T(8,128)(2,1)S(1)} %get-tuple-element.117), channel_id=1, source_target_pairs={{8,0},{16,8},{24,16},{32,24},{40,32},{48,40},{56,48},{64,56},{72,6... | collective-permute-start | bytes 221192 | tf_op jit(solution)/shard_map/ppermute | solution.py:17
  266.6 9.7 %collective-permute-start.16 = (bf16[1,22,3,384]{3,2,1,0:T(4,128)(2,1)S(1)}, bf16[1,22,3,384]{3,2,1,0:T(4,128)(2,1)S(1)}, u32[]{:S(2)}, u32[]{:S(2)}) collective-permute-start(bf16[1,22,3,384]{3,2,1,0:T(4,128)(2,1)S(1)} %get-tuple-element.112), channel_id=1, source_target_pairs={{0,1},{1,2},{2,3},{3,4},{4,5},{5,6},{6,7},{8,9},{9,10},{10,11},{11... | collective-permute-start | bytes 152072 | tf_op jit(solution)/shard_map/ppermute | solution.py:14
  271.8 6.2 %collective-permute-start.17 = (bf16[1,22,3,384]{3,2,1,0:T(4,128)(2,1)S(1)}, bf16[1,22,3,384]{3,2,1,0:T(4,128)(2,1)S(1)}, u32[]{:S(2)}, u32[]{:S(2)}) collective-permute-start(bf16[1,22,3,384]{3,2,1,0:T(4,128)(2,1)S(1)} %get-tuple-element.113), channel_id=1, source_target_pairs={{1,0},{2,1},{3,2},{4,3},{5,4},{6,5},{7,6},{9,8},{10,9},{11,10},{12... | collective-permute-start | bytes 152072 | tf_op jit(solution)/shard_map/ppermute | solution.py:17
  (193 other events, 2388.4 us)
Sparse Core Ops, SparseCore 0:
  38.0 46.8 all-gather.4
  88.0 58.7 all-gather.6
